TPU v7x, 32 devices: a whole 2x2x4 slice. The times are simulated.
32 devices in a mesh: groups: 2 (over x), col: 16 (over z, y, core).
Axes of the slice: x: 2, y: 2, z: 4, core: 2. Of those that a mesh axis runs over, the one named last changes fastest.
Arguments:
- blocks: bfloat16 [768, 128, 128], P('col'), may hold values from -0.15625 to 0.15625
- block_rows: int32 [768], P('col'), may hold values from 0 to 63, as said below
- block_cols: int32 [768], P('col'), may hold values from 0 to 127, as said below
- primal: float32 [16384, 256], P('col', 'groups'), parts along dimension 1, may hold values from -4 to 4
- dual: float32 [8192, 256], P('col', 'groups'), parts along dimension 1, may hold values from -4 to 4
- anchor_primal: float32 [16384, 256], P('col', 'groups'), parts along dimension 1, may hold values from -4 to 4
- anchor_dual: float32 [8192, 256], P('col', 'groups'), parts along dimension 1, may hold values from -4 to 4
- cost: float32 [16384, 256], P('col', 'groups'), parts along dimension 1, may hold values from -6 to 6
- rhs: float32 [8192, 256], P('col', 'groups'), parts along dimension 1, may hold values from -6 to 6
- bound_kind: int32 [16384, 256], P('col', 'groups'), parts along dimension 1, may hold values from 0 to 2
- lower: float32 [16384], P('col'), may hold values from -1.5 to -0.2
- upper: float32 [16384], P('col'), may hold values from 0.2 to 1.5
- step_size: float32 [256], P('groups'), parts along dimension 0, may hold values from 0.1 to 0.4
- primal_weight: float32 [256], P('groups'), parts along dimension 0, may hold values from 0.5 to 2
Outputs:
- primal_out: float32 [16384, 256], P('col', 'groups'), parts along dimension 1
- dual_out: float32 [8192, 256], P('col', 'groups'), parts along dimension 1
- fixed_point_residuals: float32 [3, 256], P(None, 'groups'), parts along dimension 1
There are 2 independent parts, one for each index of `groups`. A program takes and returns all parts, laid end to end along the dimension named above; an argument that names none is the same for every part. Nothing has to cross between parts.
Inputs may be any that keep to these rules, and one draw needn't show every extreme that they name: `block_rows`: the blocks 48 * d to 48 * d + 47 lie in column blocks 8 * d to 8 * d + 7, and their row blocks are among the 4 row blocks of each of d - 1, d and d + 1 (counted cyclically, row block r belonging to r // 4); no pair of row and column block appears twice. `block_cols`: see block_rows; the column blocks of entries 48 * d to 48 * d + 47 are those of d.
All inputs are finite; a program needn't handle non-finite values.
Results may differ from a plain program's by a relative error of at most 0.0015.
Values may be sent and summed in bfloat16 or wider, within the bound.
A program may use at most 64 MiB of HBM per device.

v0:
```python
import jax
import jax.numpy as jnp
from jax import lax
from jax.sharding import PartitionSpec as P

ITERS = 3


def padded(array, sides, width):
    for axis, dim in sides:
        devices, length = (lax.axis_size(axis), array.shape[dim])
        up = [(i, (i + 1) % devices) for i in range(devices)]
        down = [(j, i) for i, j in up]
        last = lax.slice_in_dim(array, length - width, length, axis=dim)
        leading = lax.slice_in_dim(array, 0, width, axis=dim)
        before = lax.ppermute(last, axis, up)
        after = lax.ppermute(leading, axis, down)
        array = jnp.concatenate([before, array, after], axis=dim)
    return array


def from_behind(block, axis, distance):
    devices = range(lax.axis_size(axis))
    route = [((i - distance) % len(devices), i) for i in devices]
    return lax.ppermute(block, axis, route)


def project_bounds(values, bound_kind, lower, upper):
    low_side = lower[:, None]
    high_side = upper[:, None]
    lower_only = jnp.maximum(values, low_side)
    boxed = jnp.minimum(jnp.maximum(values, low_side), high_side)
    return jnp.where(bound_kind == 0, values, jnp.where(bound_kind == 1, lower_only, boxed))


def per_device(
    blocks,
    block_rows,
    block_cols,
    primal,
    dual,
    anchor_primal,
    anchor_dual,
    cost,
    rhs,
    bound_kind,
    lower,
    upper,
    step_size,
    primal_weight,
):
    block_size = blocks.shape[1]
    axis_count = lax.axis_size("col")
    position = lax.axis_index("col")
    instances = primal.shape[1]
    col_blocks = primal.shape[0] // block_size
    row_blocks = dual.shape[0] // block_size
    band_blocks = 3 * row_blocks
    own_rows = dual.shape[0]
    local_rows = jnp.mod(block_rows - (position - 1) * row_blocks, row_blocks * axis_count)
    local_cols = block_cols - position * col_blocks
    primal_step = step_size / primal_weight
    dual_step = step_size * primal_weight
    cells = jnp.float32((col_blocks + row_blocks) * block_size * axis_count)
    current_x = primal
    current_y = dual
    primal_terms = []
    dual_terms = []
    for turn in range(ITERS):
        dual_rounded = current_y.astype(jnp.bfloat16)
        band_dual = padded(dual_rounded, (("col", 0),), own_rows)
        band_dual = band_dual.reshape(band_blocks, block_size, instances)
        picked = jnp.take(band_dual, local_rows, axis=0)
        products = jnp.einsum("kji,kjb->kib", blocks, picked, preferred_element_type=jnp.float32)
        gradient = (
            jnp.zeros((col_blocks, block_size, instances), jnp.float32)
            .at[local_cols]
            .add(products)
            .reshape(-1, instances)
        )
        primal_next = project_bounds(
            current_x - primal_step[None, :] * (cost - gradient), bound_kind, lower, upper
        )
        extrapolated = (
            (2.0 * primal_next - current_x)
            .astype(jnp.bfloat16)
            .reshape(col_blocks, block_size, instances)
        )
        chosen = jnp.take(extrapolated, local_cols, axis=0)
        forward = jnp.einsum("kij,kjb->kib", blocks, chosen, preferred_element_type=jnp.float32)
        partial_rows = (
            jnp.zeros((band_blocks, block_size, instances), jnp.float32)
            .at[local_rows]
            .add(forward)
            .reshape(3 * own_rows, instances)
        )
        from_upper = from_behind(partial_rows[:own_rows], "col", -1)
        from_lower = from_behind(partial_rows[2 * own_rows :], "col", 1)
        row_products = partial_rows[own_rows : 2 * own_rows] + from_upper + from_lower
        dual_next = current_y + dual_step[None, :] * (rhs - row_products)
        primal_sq = jnp.sum((primal_next - current_x) ** 2, axis=0)
        dual_sq = jnp.sum((dual_next - current_y) ** 2, axis=0)
        primal_terms.append(primal_sq)
        dual_terms.append(dual_sq)
        mixing = (turn + 1.0) / (turn + 2.0)
        current_x = mixing * (2.0 * primal_next - current_x) + (1.0 - mixing) * anchor_primal
        current_y = mixing * (2.0 * dual_next - current_y) + (1.0 - mixing) * anchor_dual
    primal_total, dual_total = lax.psum((jnp.stack(primal_terms), jnp.stack(dual_terms)), "col")
    residuals = jnp.sqrt(
        (primal_weight[None, :] * primal_total + dual_total / primal_weight[None, :]) / cells
    )
    return (current_x, current_y, residuals)


def solution(mesh):
    return jax.shard_map(
        per_device,
        mesh=mesh,
        in_specs=(
            P("col", None, None),
            P("col"),
            P("col"),
            P("col", "groups"),
            P("col", "groups"),
            P("col", "groups"),
            P("col", "groups"),
            P("col", "groups"),
            P("col", "groups"),
            P("col", "groups"),
            P("col"),
            P("col"),
            P("groups"),
            P("groups"),
        ),
        out_specs=(P("col", "groups"), P("col", "groups"), P(None, "groups")),
        check_vma=False,
    )
```

profile of v0, /device:TPU:0, one launch (start us, length us, event | category | flops | bytes accessed | tf_op | source)
XLA Modules:
  0.0 192.8 jit_solution(17058477849806929177)
XLA Ops:
  0.6 1.1 convert_element_type.18
  2.2 5.1 %collective-permute-start.1 = (bf16[512,128]{1,0:T(8,128)(2,1)S(1)}, bf16[512,128]{1,0:T(8,128)(2,1)S(1)}, u32[]{:S(2)}, u32[]{:S(2)}) collective-permute-start(bf16[512,128]{1,0:T(8,128)(2,1)S(1)} %convert_element_type.18), channel_id=1, source_target_pairs={{1,0},{2,1},{3,2},{4,3},{5,4},{6,5},{7,6},{8,7},{9,8},{10,9},{11,1... | collective-permute-start | bytes 393224 | tf_op jit(solution)/shard_map/ppermute | solution.py:17
  8.0 1.2 compare_and_fusion
  9.2 1.2 fusion.60
  11.0 0.8 gather_fusion
  11.9 2.4 %convolution_bitcast_fusion.5 = f32[48,128,128]{1,2,0:T(8,128)} fusion(bf16[48,128,128]{2,1,0:T(8,128)(2,1)S(1)} %copy-done, bf16[48,128,128]{2,1,0:T(8,128)(2,1)S(1)} %gather_fusion, pred[48]{0:T(512)(128)(4,1)S(1)} %get-tuple-element.29), kind=kOutput, calls=%fused_computation.17 | convolution fusion | flops 202113024 | bytes 6291504 | tf_op jit(solution)/shard_map/kji,kjb->kib/dot_general | solution.py:74
  14.3 3.6 %copy.24 = f32[48,128,128]{2,1,0:T(8,128)} copy(f32[48,128,128]{1,2,0:T(8,128)} %convolution_bitcast_fusion.5) | data formatting | bytes 6291456 | tf_op jit(solution)/shard_map/kji,kjb->kib/dot_general | solution.py:74
  18.0 6.7 %scatter_fusion = f32[8,128,128]{2,1,0:T(8,128)S(1)} fusion(f32[8,128,128]{2,1,0:T(8,128)S(1)} %broadcast.50.clone, s32[48]{0:T(128)S(1)} %get-tuple-element.28, f32[48,128,128]{2,1,0:T(8,128)} %copy.24), kind=kCustom, calls=%fused_computation.6 | custom fusion | flops 786432 | bytes 9437376 | tf_op jit(solution)/shard_map/scatter-add | solution.py:78
  24.8 2.7 %multiply_reduce_fusion.2 = (f32[128]{0:T(128)}, f32[1024,128]{1,0:T(8,128)S(1)}, pred[1024,128]{1,0:T(8,128)(4,1)}, pred[1024,128]{1,0:T(8,128)(4,1)}) fusion(f32[1024,128]{1,0:T(8,128)S(1)} %copy-done.9, f32[1024]{0:T(1024)S(1)} %copy-done.24, f32[1024]{0:T(1024)S(1)} %copy-done.25, f32[1024,128]{1,0:T(8,128)S(1)} %copy-done.5, ...), kind=kLoop, calls=%fused_computation.53 | loop fusion | flops 1572736 | bytes 2892800 | tf_op jit(solution)/shard_map/reduce_sum | solution.py:101
  28.2 1.1 gather_fusion.1
  29.4 3.0 %convolution_bitcast_fusion.4 = f32[48,128,128]{1,2,0:T(8,128)} fusion(bf16[48,128,128]{2,1,0:T(8,128)(2,1)S(1)} %copy-done, bf16[48,128,128]{2,1,0:T(8,128)(2,1)S(1)} %gather_fusion.1, pred[48]{0:T(512)(128)(4,1)S(1)} %copy-done.29), kind=kOutput, calls=%fused_computation.16 | convolution fusion | flops 202113024 | bytes 6291504 | tf_op jit(solution)/shard_map/kij,kjb->kib/dot_general | solution.py:90
  32.4 3.6 %copy.26 = f32[48,128,128]{2,1,0:T(8,128)} copy(f32[48,128,128]{1,2,0:T(8,128)} %convolution_bitcast_fusion.4) | data formatting | bytes 6291456 | tf_op jit(solution)/shard_map/kij,kjb->kib/dot_general | solution.py:90
  36.0 6.7 %scatter_fusion.1 = f32[12,128,128]{2,1,0:T(8,128)S(1)} fusion(f32[12,128,128]{2,1,0:T(8,128)S(1)} %broadcast.56.clone, s32[48]{0:T(128)S(1)} %get-tuple-element.30, f32[48,128,128]{2,1,0:T(8,128)} %copy.26), kind=kCustom, calls=%fused_computation.7 | custom fusion | flops 786432 | bytes 9437376 | tf_op jit(solution)/shard_map/scatter-add | solution.py:94
  42.8 3.4 %collective-permute-start.2 = (f32[512,128]{1,0:T(8,128)S(1)}, f32[512,128]{1,0:T(8,128)S(1)}, u32[]{:S(2)}, u32[]{:S(2)}) collective-permute-start(f32[512,128]{1,0:T(8,128)S(1)} %bitcast.105), channel_id=1, source_target_pairs={{1,0},{2,1},{3,2},{4,3},{5,4},{6,5},{7,6},{8,7},{9,8},{10,9},{11,1... | collective-permute-start | bytes 786440 | tf_op jit(solution)/shard_map/ppermute | solution.py:25
  46.3 3.9 %collective-permute-done.2 = f32[512,128]{1,0:T(8,128)S(1)} collective-permute-done((f32[512,128]{1,0:T(8,128)S(1)}, f32[512,128]{1,0:T(8,128)S(1)}, u32[]{:S(2)}, u32[]{:S(2)}) %collective-permute-start.2) | collective-permute-done | bytes 262176 | tf_op jit(solution)/shard_map/ppermute | solution.py:25
  50.2 4.6 %collective-permute-done.3 = f32[512,128]{1,0:T(8,128)S(1)} collective-permute-done((f32[512,128]{1,0:T(8,128)S(1)}, f32[512,128]{1,0:T(8,128)S(1)}, u32[]{:S(2)}, u32[]{:S(2)}) %collective-permute-start.3) | collective-permute-done | bytes 262176 | tf_op jit(solution)/shard_map/ppermute | solution.py:25
  55.4 0.8 fusion.56
  56.2 4.4 %collective-permute-start.5 = (bf16[512,128]{1,0:T(8,128)(2,1)S(1)}, bf16[512,128]{1,0:T(8,128)(2,1)S(1)}, u32[]{:S(2)}, u32[]{:S(2)}) collective-permute-start(bf16[512,128]{1,0:T(8,128)(2,1)S(1)} %get-tuple-element.25), channel_id=1, source_target_pairs={{1,0},{2,1},{3,2},{4,3},{5,4},{6,5},{7,6},{8,7},{9,8},{10,9},{11,1... | collective-permute-start | bytes 393224 | tf_op jit(solution)/shard_map/ppermute | solution.py:17
  60.6 2.6 %collective-permute-done.4 = bf16[512,128]{1,0:T(8,128)(2,1)S(1)} collective-permute-done((bf16[512,128]{1,0:T(8,128)(2,1)S(1)}, bf16[512,128]{1,0:T(8,128)(2,1)S(1)}, u32[]{:S(2)}, u32[]{:S(2)}) %collective-permute-start.4) | collective-permute-done | bytes 131104 | tf_op jit(solution)/shard_map/ppermute | solution.py:16
  63.3 1.0 gather_fusion.2
  64.3 3.0 %convolution_bitcast_fusion.3 = f32[48,128,128]{1,2,0:T(8,128)} fusion(bf16[48,128,128]{2,1,0:T(8,128)(2,1)S(1)} %copy-done, bf16[48,128,128]{2,1,0:T(8,128)(2,1)S(1)} %gather_fusion.2, pred[48]{0:T(512)(128)(4,1)} %copy-done.32), kind=kOutput, calls=%fused_computation.15 | convolution fusion | flops 202113024 | bytes 6291504 | tf_op jit(solution)/shard_map/kji,kjb->kib/dot_general | solution.py:74
  67.3 3.6 %copy.28 = f32[48,128,128]{2,1,0:T(8,128)} copy(f32[48,128,128]{1,2,0:T(8,128)} %convolution_bitcast_fusion.3) | data formatting | bytes 6291456 | tf_op jit(solution)/shard_map/kji,kjb->kib/dot_general | solution.py:74
  70.9 6.7 %scatter_fusion.2 = f32[8,128,128]{2,1,0:T(8,128)S(1)} fusion(f32[8,128,128]{2,1,0:T(8,128)S(1)} %broadcast.50.clone.1, s32[48]{0:T(128)S(1)} %get-tuple-element.28, f32[48,128,128]{2,1,0:T(8,128)} %copy.28), kind=kCustom, calls=%fused_computation.8 | custom fusion | flops 786432 | bytes 9437376 | tf_op jit(solution)/shard_map/scatter-add | solution.py:78
  77.7 2.2 %multiply_reduce_fusion.1 = (f32[128]{0:T(128)}, f32[1024,128]{1,0:T(8,128)S(1)}, f32[1024,128]{1,0:T(8,128)S(1)}) fusion(pred[1024,128]{1,0:T(8,128)(4,1)S(1)} %copy-done.22, pred[1024,128]{1,0:T(8,128)(4,1)S(1)} %copy-done.20, f32[1024]{0:T(1024)S(1)} %copy-done.24, f32[1024]{0:T(1024)S(1)} %copy-done.25, f32[1024,128]{1,0:T(8,128)S(1)} %copy-done.6, ...), kind=kLoop, calls=%fused_computation.52 | loop fusion | flops 1834880 | bytes 3941376 | tf_op jit(solution)/shard_map/reduce_sum | solution.py:101
  80.9 1.1 gather_fusion.3
  82.0 3.0 %convolution_bitcast_fusion.2 = f32[48,128,128]{1,2,0:T(8,128)} fusion(bf16[48,128,128]{2,1,0:T(8,128)(2,1)S(1)} %copy-done, bf16[48,128,128]{2,1,0:T(8,128)(2,1)S(1)} %gather_fusion.3, pred[48]{0:T(512)(128)(4,1)S(1)} %copy-done.30), kind=kOutput, calls=%fused_computation.14 | convolution fusion | flops 202113024 | bytes 6291504 | tf_op jit(solution)/shard_map/kij,kjb->kib/dot_general | solution.py:90
  85.0 3.6 %copy.30 = f32[48,128,128]{2,1,0:T(8,128)} copy(f32[48,128,128]{1,2,0:T(8,128)} %convolution_bitcast_fusion.2) | data formatting | bytes 6291456 | tf_op jit(solution)/shard_map/kij,kjb->kib/dot_general | solution.py:90
  88.7 6.7 %scatter_fusion.3 = f32[12,128,128]{2,1,0:T(8,128)S(1)} fusion(f32[12,128,128]{2,1,0:T(8,128)S(1)} %broadcast.56.clone.1, s32[48]{0:T(128)S(1)} %get-tuple-element.30, f32[48,128,128]{2,1,0:T(8,128)} %copy.30), kind=kCustom, calls=%fused_computation.9 | custom fusion | flops 786432 | bytes 9437376 | tf_op jit(solution)/shard_map/scatter-add | solution.py:94
  95.5 4.5 %collective-permute-start.6 = (f32[512,128]{1,0:T(8,128)S(1)}, f32[512,128]{1,0:T(8,128)S(1)}, u32[]{:S(2)}, u32[]{:S(2)}) collective-permute-start(f32[512,128]{1,0:T(8,128)S(1)} %bitcast.106), channel_id=1, source_target_pairs={{1,0},{2,1},{3,2},{4,3},{5,4},{6,5},{7,6},{8,7},{9,8},{10,9},{11,1... | collective-permute-start | bytes 786440 | tf_op jit(solution)/shard_map/ppermute | solution.py:25
  100.0 3.9 %collective-permute-done.6 = f32[512,128]{1,0:T(8,128)S(1)} collective-permute-done((f32[512,128]{1,0:T(8,128)S(1)}, f32[512,128]{1,0:T(8,128)S(1)}, u32[]{:S(2)}, u32[]{:S(2)}) %collective-permute-start.6) | collective-permute-done | bytes 262176 | tf_op jit(solution)/shard_map/ppermute | solution.py:25
  103.9 4.7 %collective-permute-done.7 = f32[512,128]{1,0:T(8,128)S(1)} collective-permute-done((f32[512,128]{1,0:T(8,128)S(1)}, f32[512,128]{1,0:T(8,128)S(1)}, u32[]{:S(2)}, u32[]{:S(2)}) %collective-permute-start.7) | collective-permute-done | bytes 262176 | tf_op jit(solution)/shard_map/ppermute | solution.py:25
  109.3 0.8 fusion.55
  110.0 4.4 %collective-permute-start.9 = (bf16[512,128]{1,0:T(8,128)(2,1)S(1)}, bf16[512,128]{1,0:T(8,128)(2,1)S(1)}, u32[]{:S(2)}, u32[]{:S(2)}) collective-permute-start(bf16[512,128]{1,0:T(8,128)(2,1)S(1)} %get-tuple-element.23), channel_id=1, source_target_pairs={{1,0},{2,1},{3,2},{4,3},{5,4},{6,5},{7,6},{8,7},{9,8},{10,9},{11,1... | collective-permute-start | bytes 393224 | tf_op jit(solution)/shard_map/ppermute | solution.py:17
  114.5 2.6 %collective-permute-done.8 = bf16[512,128]{1,0:T(8,128)(2,1)S(1)} collective-permute-done((bf16[512,128]{1,0:T(8,128)(2,1)S(1)}, bf16[512,128]{1,0:T(8,128)(2,1)S(1)}, u32[]{:S(2)}, u32[]{:S(2)}) %collective-permute-start.8) | collective-permute-done | bytes 131104 | tf_op jit(solution)/shard_map/ppermute | solution.py:16
  117.1 1.0 gather_fusion.4
  118.1 3.0 %convolution_bitcast_fusion.1 = f32[48,128,128]{1,2,0:T(8,128)} fusion(bf16[48,128,128]{2,1,0:T(8,128)(2,1)S(1)} %copy-done, bf16[48,128,128]{2,1,0:T(8,128)(2,1)S(1)} %gather_fusion.4, pred[48]{0:T(512)(128)(4,1)} %copy-done.32), kind=kOutput, calls=%fused_computation.13 | convolution fusion | flops 202113024 | bytes 6291504 | tf_op jit(solution)/shard_map/kji,kjb->kib/dot_general | solution.py:74
  121.1 3.6 %copy.32 = f32[48,128,128]{2,1,0:T(8,128)} copy(f32[48,128,128]{1,2,0:T(8,128)} %convolution_bitcast_fusion.1) | data formatting | bytes 6291456 | tf_op jit(solution)/shard_map/kji,kjb->kib/dot_general | solution.py:74
  124.8 6.7 %scatter_fusion.4 = f32[8,128,128]{2,1,0:T(8,128)S(1)} fusion(f32[8,128,128]{2,1,0:T(8,128)S(1)} %broadcast.50, s32[48]{0:T(128)S(1)} %get-tuple-element.28, f32[48,128,128]{2,1,0:T(8,128)} %copy.32), kind=kCustom, calls=%fused_computation.10 | custom fusion | flops 786432 | bytes 9437376 | tf_op jit(solution)/shard_map/scatter-add | solution.py:78
  131.6 1.7 multiply_reduce_fusion
  133.2 0.9 fusion.41
  134.1 1.1 gather_fusion.5
  135.2 3.0 %convolution_bitcast_fusion = f32[48,128,128]{1,2,0:T(8,128)} fusion(bf16[48,128,128]{2,1,0:T(8,128)(2,1)S(1)} %copy-done, bf16[48,128,128]{2,1,0:T(8,128)(2,1)S(1)} %gather_fusion.5, pred[48]{0:T(512)(128)(4,1)S(1)} %copy-done.31), kind=kOutput, calls=%fused_computation.12 | convolution fusion | flops 202113024 | bytes 6291504 | tf_op jit(solution)/shard_map/kij,kjb->kib/dot_general | solution.py:90
  138.2 3.6 %copy.34 = f32[48,128,128]{2,1,0:T(8,128)} copy(f32[48,128,128]{1,2,0:T(8,128)} %convolution_bitcast_fusion) | data formatting | bytes 6291456 | tf_op jit(solution)/shard_map/kij,kjb->kib/dot_general | solution.py:90
  141.9 6.7 %scatter_fusion.5 = f32[12,128,128]{2,1,0:T(8,128)S(1)} fusion(f32[12,128,128]{2,1,0:T(8,128)S(1)} %broadcast.56, s32[48]{0:T(128)S(1)} %get-tuple-element.30, f32[48,128,128]{2,1,0:T(8,128)} %copy.34), kind=kCustom, calls=%fused_computation.11 | custom fusion | flops 786432 | bytes 9437376 | tf_op jit(solution)/shard_map/scatter-add | solution.py:94
  148.8 4.5 %collective-permute-start.10 = (f32[512,128]{1,0:T(8,128)S(1)}, f32[512,128]{1,0:T(8,128)S(1)}, u32[]{:S(2)}, u32[]{:S(2)}) collective-permute-start(f32[512,128]{1,0:T(8,128)S(1)} %bitcast.107), channel_id=1, source_target_pairs={{1,0},{2,1},{3,2},{4,3},{5,4},{6,5},{7,6},{8,7},{9,8},{10,9},{11,1... | collective-permute-start | bytes 786440 | tf_op jit(solution)/shard_map/ppermute | solution.py:25
  153.3 3.9 %collective-permute-done.10 = f32[512,128]{1,0:T(8,128)S(1)} collective-permute-done((f32[512,128]{1,0:T(8,128)S(1)}, f32[512,128]{1,0:T(8,128)S(1)}, u32[]{:S(2)}, u32[]{:S(2)}) %collective-permute-start.10) | collective-permute-done | bytes 262176 | tf_op jit(solution)/shard_map/ppermute | solution.py:25
  157.2 4.6 %collective-permute-done.11 = f32[512,128]{1,0:T(8,128)S(1)} collective-permute-done((f32[512,128]{1,0:T(8,128)S(1)}, f32[512,128]{1,0:T(8,128)S(1)}, u32[]{:S(2)}, u32[]{:S(2)}) %collective-permute-start.11) | collective-permute-done | bytes 262176 | tf_op jit(solution)/shard_map/ppermute | solution.py:25
  162.7 29.5 %all-reduce = (f32[3,128]{1,0:T(4,128)S(1)}, f32[3,128]{1,0:T(4,128)S(1)}) all-reduce(f32[3,128]{1,0:T(4,128)S(1)} %get-tuple-element.45, f32[3,128]{1,0:T(4,128)S(1)} %get-tuple-element.44), channel_id=1, replica_groups=mesh['groups'=2,'col'=16] {'col'}, use_global_device_ids=true, to_apply=%region_13.16 | all-reduce | flops 768 | bytes 6144 | tf_op jit(solution)/shard_map/psum | solution.py:108
  (117 shorter events, 7.0 us)
Async XLA Ops:
  0.6 11.3 %copy-start = (bf16[48,128,128]{2,1,0:T(8,128)(2,1)S(1)}, bf16[48,128,128]{2,1,0:T(8,128)(2,1)}, u32[]{:S(2)}) copy-start(bf16[48,128,128]{2,1,0:T(8,128)(2,1)} %param.18) | copy-start | bytes 4718596
  1.7 9.3 %collective-permute-start = (bf16[512,128]{1,0:T(8,128)(2,1)S(1)}, bf16[512,128]{1,0:T(8,128)(2,1)S(1)}, u32[]{:S(2)}, u32[]{:S(2)}) collective-permute-start(bf16[512,128]{1,0:T(8,128)(2,1)S(1)} %convert_element_type.18), channel_id=1, source_target_pairs={{0,1},{1,2},{2,3},{3,4},{4,5},{5,6},{6,7},{7,8},{8,9},{9,10},{10,1... | collective-permute-start | bytes 393224 | tf_op jit(solution)/shard_map/ppermute | solution.py:16
  2.2 8.8 %collective-permute-start.1 = (bf16[512,128]{1,0:T(8,128)(2,1)S(1)}, bf16[512,128]{1,0:T(8,128)(2,1)S(1)}, u32[]{:S(2)}, u32[]{:S(2)}) collective-permute-start(bf16[512,128]{1,0:T(8,128)(2,1)S(1)} %convert_element_type.18), channel_id=1, source_target_pairs={{1,0},{2,1},{3,2},{4,3},{5,4},{6,5},{7,6},{8,7},{9,8},{10,9},{11,1... | collective-permute-start | bytes 393224 | tf_op jit(solution)/shard_map/ppermute | solution.py:17
  8.0 3.9 %copy-start.32 = (pred[48]{0:T(512)(128)(4,1)}, pred[48]{0:T(512)(128)(4,1)S(1)}, u32[]{:S(2)}) copy-start(pred[48]{0:T(512)(128)(4,1)S(1)} %get-tuple-element.29) | copy-start | bytes 148
  10.4 1.5 copy-start.36
  17.9 6.8 %copy-start.5 = (f32[1024,128]{1,0:T(8,128)S(1)}, f32[1024,128]{1,0:T(8,128)}, u32[]{:S(2)}) copy-start(f32[1024,128]{1,0:T(8,128)} %param.25) | copy-start | bytes 1572868
  17.9 6.8 %copy-start.9 = (f32[1024,128]{1,0:T(8,128)S(1)}, f32[1024,128]{1,0:T(8,128)}, u32[]{:S(2)}) copy-start(f32[1024,128]{1,0:T(8,128)} %param.21) | copy-start | bytes 1572868
  18.0 6.8 %copy-start.24 = (f32[1024]{0:T(1024)S(1)}, f32[1024]{0:T(1024)}, u32[]{:S(2)}) copy-start(f32[1024]{0:T(1024)} %param.29) | copy-start | bytes 12292
  18.0 6.8 %copy-start.25 = (f32[1024]{0:T(1024)S(1)}, f32[1024]{0:T(1024)}, u32[]{:S(2)}) copy-start(f32[1024]{0:T(1024)} %param.28) | copy-start | bytes 12292
  18.0 6.8 %copy-start.33 = (f32[128]{0:T(128)S(1)}, f32[128]{0:T(128)}, u32[]{:S(2)}) copy-start(f32[128]{0:T(128)} %get-tuple-element.43) | copy-start | bytes 1540
  42.7 12.0 %copy-start.11 = (f32[512,128]{1,0:T(8,128)S(1)}, f32[512,128]{1,0:T(8,128)}, u32[]{:S(2)}) copy-start(f32[512,128]{1,0:T(8,128)} %param.22) | copy-start | bytes 786436
  42.7 12.0 %copy-start.12 = (f32[512,128]{1,0:T(8,128)S(1)}, f32[512,128]{1,0:T(8,128)}, u32[]{:S(2)}) copy-start(f32[512,128]{1,0:T(8,128)} %param.26) | copy-start | bytes 786436
  42.7 12.0 %copy-start.26 = (f32[128]{0:T(128)S(1)}, f32[128]{0:T(128)}, u32[]{:S(2)}) copy-start(f32[128]{0:T(128)} %get-tuple-element.42) | copy-start | bytes 1540
  42.7 12.7 %copy-start.15 = (f32[512,128]{1,0:T(8,128)S(1)}, f32[512,128]{1,0:T(8,128)}, u32[]{:S(2)}) copy-start(f32[512,128]{1,0:T(8,128)} %param.24) | copy-start | bytes 786436
  42.8 7.3 %collective-permute-start.2 = (f32[512,128]{1,0:T(8,128)S(1)}, f32[512,128]{1,0:T(8,128)S(1)}, u32[]{:S(2)}, u32[]{:S(2)}) collective-permute-start(f32[512,128]{1,0:T(8,128)S(1)} %bitcast.105), channel_id=1, source_target_pairs={{1,0},{2,1},{3,2},{4,3},{5,4},{6,5},{7,6},{8,7},{9,8},{10,9},{11,1... | collective-permute-start | bytes 786440 | tf_op jit(solution)/shard_map/ppermute | solution.py:25
  46.3 8.5 %collective-permute-start.3 = (f32[512,128]{1,0:T(8,128)S(1)}, f32[512,128]{1,0:T(8,128)S(1)}, u32[]{:S(2)}, u32[]{:S(2)}) collective-permute-start(f32[512,128]{1,0:T(8,128)S(1)} %bitcast.102), channel_id=1, source_target_pairs={{15,0},{0,1},{1,2},{2,3},{3,4},{4,5},{5,6},{6,7},{7,8},{8,9},{9,10... | collective-permute-start | bytes 786440 | tf_op jit(solution)/shard_map/ppermute | solution.py:25
  56.2 7.1 %collective-permute-start.4 = (bf16[512,128]{1,0:T(8,128)(2,1)S(1)}, bf16[512,128]{1,0:T(8,128)(2,1)S(1)}, u32[]{:S(2)}, u32[]{:S(2)}) collective-permute-start(bf16[512,128]{1,0:T(8,128)(2,1)S(1)} %get-tuple-element.25), channel_id=1, source_target_pairs={{0,1},{1,2},{2,3},{3,4},{4,5},{5,6},{6,7},{7,8},{8,9},{9,10},{10,1... | collective-permute-start | bytes 393224 | tf_op jit(solution)/shard_map/ppermute | solution.py:16
  56.2 7.1 %collective-permute-start.5 = (bf16[512,128]{1,0:T(8,128)(2,1)S(1)}, bf16[512,128]{1,0:T(8,128)(2,1)S(1)}, u32[]{:S(2)}, u32[]{:S(2)}) collective-permute-start(bf16[512,128]{1,0:T(8,128)(2,1)S(1)} %get-tuple-element.25), channel_id=1, source_target_pairs={{1,0},{2,1},{3,2},{4,3},{5,4},{6,5},{7,6},{8,7},{9,8},{10,9},{11,1... | collective-permute-start | bytes 393224 | tf_op jit(solution)/shard_map/ppermute | solution.py:17
  70.9 6.8 %copy-start.6 = (f32[1024,128]{1,0:T(8,128)S(1)}, f32[1024,128]{1,0:T(8,128)}, u32[]{:S(2)}) copy-start(f32[1024,128]{1,0:T(8,128)} %param.25) | copy-start | bytes 1572868
  70.9 6.8 %copy-start.7 = (f32[1024,128]{1,0:T(8,128)S(1)}, f32[1024,128]{1,0:T(8,128)}, u32[]{:S(2)}) copy-start(f32[1024,128]{1,0:T(8,128)} %param.23) | copy-start | bytes 1572868
  70.9 6.8 %copy-start.20 = (pred[1024,128]{1,0:T(8,128)(4,1)S(1)}, pred[1024,128]{1,0:T(8,128)(4,1)}, u32[]{:S(2)}) copy-start(pred[1024,128]{1,0:T(8,128)(4,1)} %get-tuple-element.9) | copy-start | bytes 393220
  70.9 6.8 %copy-start.22 = (pred[1024,128]{1,0:T(8,128)(4,1)S(1)}, pred[1024,128]{1,0:T(8,128)(4,1)}, u32[]{:S(2)}) copy-start(pred[1024,128]{1,0:T(8,128)(4,1)} %get-tuple-element.10) | copy-start | bytes 393220
  70.9 6.8 %copy-start.34 = (f32[128]{0:T(128)S(1)}, f32[128]{0:T(128)}, u32[]{:S(2)}) copy-start(f32[128]{0:T(128)} %get-tuple-element.43) | copy-start | bytes 1540
  95.4 13.2 %copy-start.13 = (f32[512,128]{1,0:T(8,128)S(1)}, f32[512,128]{1,0:T(8,128)}, u32[]{:S(2)}) copy-start(f32[512,128]{1,0:T(8,128)} %param.26) | copy-start | bytes 786436
  95.4 13.2 %copy-start.19 = (f32[512,128]{1,0:T(8,128)S(1)}, f32[512,128]{1,0:T(8,128)}, u32[]{:S(2)}) copy-start(f32[512,128]{1,0:T(8,128)} %get-tuple-element.26) | copy-start | bytes 786436
  95.4 13.2 %copy-start.27 = (f32[128]{0:T(128)S(1)}, f32[128]{0:T(128)}, u32[]{:S(2)}) copy-start(f32[128]{0:T(128)} %get-tuple-element.42) | copy-start | bytes 1540
  95.4 13.8 %copy-start.16 = (f32[512,128]{1,0:T(8,128)S(1)}, f32[512,128]{1,0:T(8,128)}, u32[]{:S(2)}) copy-start(f32[512,128]{1,0:T(8,128)} %param.24) | copy-start | bytes 786436
  95.5 8.4 %collective-permute-start.6 = (f32[512,128]{1,0:T(8,128)S(1)}, f32[512,128]{1,0:T(8,128)S(1)}, u32[]{:S(2)}, u32[]{:S(2)}) collective-permute-start(f32[512,128]{1,0:T(8,128)S(1)} %bitcast.106), channel_id=1, source_target_pairs={{1,0},{2,1},{3,2},{4,3},{5,4},{6,5},{7,6},{8,7},{9,8},{10,9},{11,1... | collective-permute-start | bytes 786440 | tf_op jit(solution)/shard_map/ppermute | solution.py:25
  100.0 8.6 %collective-permute-start.7 = (f32[512,128]{1,0:T(8,128)S(1)}, f32[512,128]{1,0:T(8,128)S(1)}, u32[]{:S(2)}, u32[]{:S(2)}) collective-permute-start(f32[512,128]{1,0:T(8,128)S(1)} %bitcast.103), channel_id=1, source_target_pairs={{15,0},{0,1},{1,2},{2,3},{3,4},{4,5},{5,6},{6,7},{7,8},{8,9},{9,10... | collective-permute-start | bytes 786440 | tf_op jit(solution)/shard_map/ppermute | solution.py:25
  110.0 7.1 %collective-permute-start.8 = (bf16[512,128]{1,0:T(8,128)(2,1)S(1)}, bf16[512,128]{1,0:T(8,128)(2,1)S(1)}, u32[]{:S(2)}, u32[]{:S(2)}) collective-permute-start(bf16[512,128]{1,0:T(8,128)(2,1)S(1)} %get-tuple-element.23), channel_id=1, source_target_pairs={{0,1},{1,2},{2,3},{3,4},{4,5},{5,6},{6,7},{7,8},{8,9},{9,10},{10,1... | collective-permute-start | bytes 393224 | tf_op jit(solution)/shard_map/ppermute | solution.py:16
  110.0 7.1 %collective-permute-start.9 = (bf16[512,128]{1,0:T(8,128)(2,1)S(1)}, bf16[512,128]{1,0:T(8,128)(2,1)S(1)}, u32[]{:S(2)}, u32[]{:S(2)}) collective-permute-start(bf16[512,128]{1,0:T(8,128)(2,1)S(1)} %get-tuple-element.23), channel_id=1, source_target_pairs={{1,0},{2,1},{3,2},{4,3},{5,4},{6,5},{7,6},{8,7},{9,8},{10,9},{11,1... | collective-permute-start | bytes 393224 | tf_op jit(solution)/shard_map/ppermute | solution.py:17
  124.7 6.8 %copy-start.2 = (f32[1024,128]{1,0:T(8,128)S(1)}, f32[1024,128]{1,0:T(8,128)}, u32[]{:S(2)}) copy-start(f32[1024,128]{1,0:T(8,128)} %copy-done.1) | copy-start | bytes 1572868
  124.7 6.8 %copy-start.4 = (f32[1024,128]{1,0:T(8,128)S(1)}, f32[1024,128]{1,0:T(8,128)}, u32[]{:S(2)}) copy-start(f32[1024,128]{1,0:T(8,128)} %copy-done.3) | copy-start | bytes 1572868
  124.7 6.8 %copy-start.21 = (pred[1024,128]{1,0:T(8,128)(4,1)S(1)}, pred[1024,128]{1,0:T(8,128)(4,1)}, u32[]{:S(2)}) copy-start(pred[1024,128]{1,0:T(8,128)(4,1)} %get-tuple-element.9) | copy-start | bytes 393220
  124.8 6.8 %copy-start.23 = (pred[1024,128]{1,0:T(8,128)(4,1)S(1)}, pred[1024,128]{1,0:T(8,128)(4,1)}, u32[]{:S(2)}) copy-start(pred[1024,128]{1,0:T(8,128)(4,1)} %get-tuple-element.10) | copy-start | bytes 393220
  124.8 6.8 %copy-start.35 = (f32[128]{0:T(128)S(1)}, f32[128]{0:T(128)}, u32[]{:S(2)}) copy-start(f32[128]{0:T(128)} %get-tuple-element.43) | copy-start | bytes 1540
  131.6 1.7 copy-start.8
  148.6 13.2 %copy-start.14 = (f32[512,128]{1,0:T(8,128)S(1)}, f32[512,128]{1,0:T(8,128)}, u32[]{:S(2)}) copy-start(f32[512,128]{1,0:T(8,128)} %param.26) | copy-start | bytes 786436
  148.6 13.2 %copy-start.18 = (f32[512,128]{1,0:T(8,128)S(1)}, f32[512,128]{1,0:T(8,128)}, u32[]{:S(2)}) copy-start(f32[512,128]{1,0:T(8,128)} %get-tuple-element.24) | copy-start | bytes 786436
  148.6 13.2 %copy-start.28 = (f32[128]{0:T(128)S(1)}, f32[128]{0:T(128)}, u32[]{:S(2)}) copy-start(f32[128]{0:T(128)} %get-tuple-element.42) | copy-start | bytes 1540
  148.6 13.3 %copy-start.17 = (f32[512,128]{1,0:T(8,128)S(1)}, f32[512,128]{1,0:T(8,128)}, u32[]{:S(2)}) copy-start(f32[512,128]{1,0:T(8,128)} %param.24) | copy-start | bytes 786436
  148.7 13.9 %copy-start.37 = (f32[128]{0:T(128)S(1)}, f32[128]{0:T(128)}, u32[]{:S(2)}) copy-start(f32[128]{0:T(128)} %get-tuple-element.17) | copy-start | bytes 1540
  148.7 13.9 %copy-start.38 = (f32[128]{0:T(128)S(1)}, f32[128]{0:T(128)}, u32[]{:S(2)}) copy-start(f32[128]{0:T(128)} %get-tuple-element.11) | copy-start | bytes 1540
  148.7 13.9 %copy-start.39 = (f32[128]{0:T(128)S(1)}, f32[128]{0:T(128)}, u32[]{:S(2)}) copy-start(f32[128]{0:T(128)} %get-tuple-element.19) | copy-start | bytes 1540
  148.7 13.9 %copy-start.41 = (f32[128]{0:T(128)S(1)}, f32[128]{0:T(128)}, u32[]{:S(2)}) copy-start(f32[128]{0:T(128)} %get-tuple-element.7) | copy-start | bytes 1540
  148.8 43.4 %copy-start.40 = (f32[128]{0:T(128)S(1)}, f32[128]{0:T(128)}, u32[]{:S(2)}) copy-start(f32[128]{0:T(128)} %param.31) | copy-start | bytes 1540
  148.8 8.4 %collective-permute-start.10 = (f32[512,128]{1,0:T(8,128)S(1)}, f32[512,128]{1,0:T(8,128)S(1)}, u32[]{:S(2)}, u32[]{:S(2)}) collective-permute-start(f32[512,128]{1,0:T(8,128)S(1)} %bitcast.107), channel_id=1, source_target_pairs={{1,0},{2,1},{3,2},{4,3},{5,4},{6,5},{7,6},{8,7},{9,8},{10,9},{11,1... | collective-permute-start | bytes 786440 | tf_op jit(solution)/shard_map/ppermute | solution.py:25
  153.3 8.5 %collective-permute-start.11 = (f32[512,128]{1,0:T(8,128)S(1)}, f32[512,128]{1,0:T(8,128)S(1)}, u32[]{:S(2)}, u32[]{:S(2)}) collective-permute-start(f32[512,128]{1,0:T(8,128)S(1)} %bitcast.104), channel_id=1, source_target_pairs={{15,0},{0,1},{1,2},{2,3},{3,4},{4,5},{5,6},{6,7},{7,8},{8,9},{9,10... | collective-permute-start | bytes 786440 | tf_op jit(solution)/shard_map/ppermute | solution.py:25
  (6 other events, 5.9 us)
where the time goes:
time: 194 us; the launch traced here: 193 us
  other arithmetic  57 us (29%)
  waiting for transfers between devices  30.9 us (16%)
  local copies, waits for them, and re-layouts  29.8 us (15%)
  blocking collectives  29.5 us (15%)
  starting transfers between devices  26.9 us (14%)
  matrix products  17.4 us (9%)
    psum x1, blocking collectives, per_device(): lax.psum((jnp.stack(primal_terms), jnp.stack(dual_terms)), 'col')  29.5 us
    ppermute x6, waiting for transfers between devices, from_behind(): return lax.ppermute(block, axis, route)  25.6 us
    scatter-add x3, other arithmetic, per_device(): gradient = jnp.zeros((col_blocks, block_size, instances), jnp.float32).at...  20.2 us
    scatter-add x3, other arithmetic, per_device(): partial_rows = jnp.zeros((band_blocks, block_size, instances), jnp.float3...  20.2 us
    ppermute x3, starting transfers between devices, padded(): after = lax.ppermute(leading, axis, down)  13.9 us
    ppermute x6, starting transfers between devices, from_behind(): return lax.ppermute(block, axis, route)  12.4 us
    dot_general x3, local copies, waits for them, and re-layouts, per_device(): jnp.einsum('kji,kjb->kib', blocks, picked, preferred_element_type=jnp.flo...  10.7 us
    dot_general x3, local copies, waits for them, and re-layouts, per_device(): jnp.einsum('kij,kjb->kib', blocks, chosen, preferred_element_type=jnp.flo...  10.7 us
  transfers between devices with their start and end apart: 12, of which 8 were waited for; matrix products, arithmetic and copies ran while one was open for 2% of the time, Pallas kernels for 0%

commit v1 on v0

v1 whole, which is shorter than its diff:
```python
import functools

import jax
import jax.numpy as jnp
from jax import lax
from jax.experimental import pallas as pl
from jax.experimental.pallas import tpu as pltpu
from jax.sharding import PartitionSpec as P

ITERS = 3
CHUNKS = 2
FAR, NEAR, OWN = 0, 1, 2
MESH = pl.DeviceIdType.MESH


def kernel(
    n,
    blocks_hbm,
    rows_hbm,
    cols_hbm,
    primal_hbm,
    dual_hbm,
    anchor_primal_hbm,
    anchor_dual_hbm,
    cost_hbm,
    rhs_hbm,
    kind_hbm,
    lower_hbm,
    upper_hbm,
    step_hbm,
    weight_hbm,
    primal_out,
    dual_out,
    residual_out,
    blk,
    blk_t,
    rows,
    cols,
    table_v,
    table,
    mat,
    mat_t,
    x,
    x_next,
    anchor_x,
    cost,
    kind,
    low,
    high,
    low_rows,
    high_rows,
    grad,
    extra,
    y,
    anchor_y,
    rhs,
    own_y,
    halo,
    row_own,
    far_send,
    far_recv,
    near_send,
    near_recv,
    step,
    weight,
    res_send,
    res_recv,
    res,
    load_sem,
    store_sem,
    halo_send_sem,
    halo_recv_sem,
    part_send_sem,
    part_recv_sem,
    res_send_sem,
    res_recv_sem,
    table_sem,
):
    me = lax.axis_index("col")
    nz, size, _ = blocks_hbm.shape
    ncols, nrows = x.shape[0], y.shape[0]
    row_blocks, col_blocks = nrows // size, ncols // size
    part = nrows // CHUNKS
    parity = lax.rem(me, 2)
    far_dev = lax.rem(me + 2 * parity - 1 + n, n)
    near_dev = lax.rem(me + 1 - 2 * parity + n, n)
    partner = (far_dev, near_dev)

    barrier = pltpu.get_barrier_semaphore()

    def greet(k, carry):
        pl.semaphore_signal(barrier, inc=1, device_id={"col": lax.rem(me + k, n)}, device_id_type=MESH)
        return carry

    lax.fori_loop(1, n, greet, 0)

    loads = {}
    for place, (name, source, target) in enumerate(
        (
            ("y", dual_hbm, y),
            ("rows", rows_hbm, rows),
            ("cols", cols_hbm, cols),
            ("blocks", blocks_hbm, blk.at[pl.ds(1, nz)]),
            ("low", lower_hbm, low_rows),
            ("high", upper_hbm, high_rows),
            ("step", step_hbm, step),
            ("weight", weight_hbm, weight),
            ("x", primal_hbm, x),
            ("cost", cost_hbm, cost),
            ("kind", kind_hbm, kind),
            ("rhs", rhs_hbm, rhs),
            ("anchor_x", anchor_primal_hbm, anchor_x),
            ("anchor_y", anchor_dual_hbm, anchor_y),
        )
    ):
        loads[name] = pltpu.make_async_copy(source, target, load_sem.at[place])
        loads[name].start()

    def halo_copy(turn, who, c):
        return pltpu.make_async_remote_copy(
            src_ref=own_y.at[turn, c],
            dst_ref=halo.at[turn, who, c],
            send_sem=halo_send_sem.at[turn, who, c],
            recv_sem=halo_recv_sem.at[turn, who, c],
            device_id={"col": partner[who]},
            device_id_type=MESH,
        )

    part_send, part_recv = (far_send, near_send), (far_recv, near_recv)

    def part_copy(turn, who, c):
        return pltpu.make_async_remote_copy(
            src_ref=part_send[who].at[turn, c],
            dst_ref=part_recv[who].at[turn, c],
            send_sem=part_send_sem.at[turn, who, c],
            recv_sem=part_recv_sem.at[turn, who, c],
            device_id={"col": partner[who]},
            device_id_type=MESH,
        )

    sent = []
    loads["y"].wait()
    for c in range(CHUNKS):
        own_y[0, c] = y[c * part : (c + 1) * part].astype(jnp.bfloat16)
    pl.semaphore_wait(barrier, n - 1)
    for c in range(CHUNKS):
        for who in (FAR, NEAR):
            copy = halo_copy(0, who, c)
            copy.start()
            sent.append(copy)

    loads["rows"].wait()
    loads["cols"].wait()
    local_row = rows[...] - (me - 1) * row_blocks
    local_row = jnp.where(local_row < 0, local_row + row_blocks * n, local_row)
    local_row = jnp.where(local_row >= row_blocks * n, local_row - row_blocks * n, local_row)
    segment = jnp.where(local_row >= 2 * row_blocks, 2, jnp.where(local_row >= row_blocks, 1, 0))
    owner = jnp.where(segment == 1, OWN, jnp.where(segment == 2 * parity, FAR, NEAR))
    band_row = local_row + (owner - segment) * row_blocks
    place = band_row * col_blocks + cols[...] - me * col_blocks
    match = lax.broadcasted_iota(jnp.int32, (128, nz), 0) == place
    number = lax.broadcasted_iota(jnp.int32, (128, nz), 1) + 1
    found = jnp.max(jnp.where(match, number, 0), axis=1, keepdims=True)
    table_v[...] = jnp.transpose(jnp.broadcast_to(found, (128, 128)))[0:1]
    to_scalar = pltpu.make_async_copy(table_v, table, table_sem)
    to_scalar.start()

    loads["low"].wait()
    loads["high"].wait()
    for c in range(col_blocks):
        span = slice(c * size, (c + 1) * size)
        low[span] = jnp.transpose(jnp.broadcast_to(low_rows[c : c + 1], (size, x.shape[1])))
        high[span] = jnp.transpose(jnp.broadcast_to(high_rows[c : c + 1], (size, x.shape[1])))

    blk[0] = jnp.zeros((size, size), jnp.bfloat16)
    blk_t[0] = jnp.zeros((size, size), jnp.bfloat16)
    loads["blocks"].wait()

    def turn_block(k, carry):
        blk_t[k] = jnp.transpose(blk[k])
        return carry

    lax.fori_loop(1, nz + 1, turn_block, 0, unroll=4)
    to_scalar.wait()

    def build(r, carry):
        down = pl.ds(pl.multiple_of(r * size, size), size)
        for c in range(col_blocks):
            which = table[0, r * col_blocks + c]
            mat[down, c * size : (c + 1) * size] = blk[which]
            mat_t[c * size : (c + 1) * size, down] = blk_t[which]
        return carry

    lax.fori_loop(0, 3 * row_blocks, build, 0)

    loads["step"].wait()
    loads["weight"].wait()
    primal_step = step[...] / weight[...]
    dual_step = step[...] * weight[...]
    res_send[...] = jnp.zeros_like(res_send)
    for name in ("x", "cost", "kind"):
        loads[name].wait()

    def times(left, right):
        return jnp.dot(left, right, preferred_element_type=jnp.float32)

    width = 256
    for turn in range(ITERS):
        first = {FAR: 0, NEAR: nrows, OWN: 2 * nrows}
        grad[...] = times(
            mat_t[:, 2 * nrows : 3 * nrows],
            jnp.concatenate([own_y[turn, c] for c in range(CHUNKS)], axis=0),
        )
        order = [(NEAR, c) for c in range(CHUNKS)] + [(FAR, c) for c in range(CHUNKS)]
        for who, c in order[:-1]:
            halo_copy(turn, who, c).wait_recv()
            at = first[who] + c * part
            grad[...] += times(mat_t[:, at : at + part], halo[turn, who, c])
        who, c = order[-1]
        halo_copy(turn, who, c).wait_recv()
        at = first[who] + c * part
        for i in range(0, ncols, width):
            span = slice(i, i + width)
            total = grad[span] + times(mat_t[span, at : at + part], halo[turn, who, c])
            now = x[span]
            value = now - primal_step * (cost[span] - total)
            of_kind = kind[span]
            lower_only = jnp.maximum(value, low[span])
            boxed = jnp.minimum(lower_only, high[span])
            after = jnp.where(of_kind == 0, value, jnp.where(of_kind == 1, lower_only, boxed))
            x_next[span] = after
            extra[span] = (2.0 * after - now).astype(jnp.bfloat16)

        for who in (FAR, NEAR):
            for c in range(CHUNKS):
                at = first[who] + c * part
                part_send[who][turn, c] = times(mat[at : at + part], extra[...]).astype(part_send[who].dtype)
                copy = part_copy(turn, who, c)
                copy.start()
                sent.append(copy)
        row_own[...] = times(mat[2 * nrows :], extra[...])

        mixing = (turn + 1.0) / (turn + 2.0)
        if turn == 0:
            loads["anchor_x"].wait()
        primal_sq = jnp.zeros((1, x.shape[1]), jnp.float32)
        for i in range(0, ncols, width):
            span = slice(i, i + width)
            now, after = x[span], x_next[span]
            primal_sq += jnp.sum((after - now) ** 2, axis=0, keepdims=True)
            x[span] = mixing * (2.0 * after - now) + (1.0 - mixing) * anchor_x[span]
        if turn == ITERS - 1:
            x_store = pltpu.make_async_copy(x, primal_out, store_sem.at[0])
            x_store.start()

        if turn == 0:
            loads["rhs"].wait()
            loads["anchor_y"].wait()
        dual_sq = jnp.zeros((1, x.shape[1]), jnp.float32)
        for c in range(CHUNKS):
            span = slice(c * part, (c + 1) * part)
            part_copy(turn, NEAR, c).wait_recv()
            part_copy(turn, FAR, c).wait_recv()
            products = (
                row_own[span]
                + near_recv[turn, c]
                + far_recv[turn, c].astype(jnp.float32)
            )
            now = y[span]
            after = now + dual_step * (rhs[span] - products)
            new = mixing * (2.0 * after - now) + (1.0 - mixing) * anchor_y[span]
            y[span] = new
            if turn < ITERS - 1:
                own_y[turn + 1, c] = new.astype(jnp.bfloat16)
                for who in (FAR, NEAR):
                    copy = halo_copy(turn + 1, who, c)
                    copy.start()
                    sent.append(copy)
            dual_sq += jnp.sum((after - now) ** 2, axis=0, keepdims=True)
        res_send[turn : turn + 1] = weight[...] * primal_sq + dual_sq / weight[...]

    def res_copy(k):
        return pltpu.make_async_remote_copy(
            src_ref=res_send,
            dst_ref=res_recv.at[k],
            send_sem=res_send_sem.at[k],
            recv_sem=res_recv_sem.at[k],
            device_id={"col": lax.rem(me + k, n)},
            device_id_type=MESH,
        )

    def spread(k, carry):
        res_copy(k).start()
        return carry

    lax.fori_loop(1, n, spread, 0)
    y_store = pltpu.make_async_copy(y, dual_out, store_sem.at[1])
    y_store.start()
    res_recv[0] = res_send[...]
    for copy in sent:
        copy.wait_send()

    def collect(k, carry):
        res_copy(k).wait()
        return carry

    lax.fori_loop(1, n, collect, 0)
    total = jnp.sum(res_recv[...], axis=0)
    cells = jnp.float32((ncols + nrows) * n)
    res[...] = jnp.sqrt(total[0:ITERS] / cells)
    res_store = pltpu.make_async_copy(res, residual_out, store_sem.at[2])
    res_store.start()
    x_store.wait()
    y_store.wait()
    res_store.wait()


def per_device(
    blocks,
    block_rows,
    block_cols,
    primal,
    dual,
    anchor_primal,
    anchor_dual,
    cost,
    rhs,
    bound_kind,
    lower,
    upper,
    step_size,
    primal_weight,
):
    n = lax.axis_size("col")
    nz, size, _ = blocks.shape
    ncols, inst = primal.shape
    nrows = dual.shape[0]
    part = nrows // CHUNKS
    f32, bf16, i32 = jnp.float32, jnp.bfloat16, jnp.int32
    any_space = pl.BlockSpec(memory_space=pl.ANY)
    vmem = pltpu.VMEM
    dma = pltpu.SemaphoreType.DMA
    return pl.pallas_call(
        functools.partial(kernel, n),
        out_shape=(
            jax.ShapeDtypeStruct((ncols, inst), f32),
            jax.ShapeDtypeStruct((nrows, inst), f32),
            jax.ShapeDtypeStruct((ITERS, inst), f32),
        ),
        in_specs=[any_space] * 14,
        out_specs=(any_space,) * 3,
        scratch_shapes=[
            vmem((nz + 1, size, size), bf16),
            vmem((nz + 1, size, size), bf16),
            vmem((1, nz), i32),
            vmem((1, nz), i32),
            vmem((1, 128), i32),
            pltpu.SMEM((1, 128), i32),
            vmem((3 * nrows, ncols), bf16),
            vmem((ncols, 3 * nrows), bf16),
            vmem((ncols, inst), f32),
            vmem((ncols, inst), f32),
            vmem((ncols, inst), f32),
            vmem((ncols, inst), f32),
            vmem((ncols, inst), i32),
            vmem((ncols, inst), f32),
            vmem((ncols, inst), f32),
            vmem((ncols // size, size), f32),
            vmem((ncols // size, size), f32),
            vmem((ncols, inst), f32),
            vmem((ncols, inst), bf16),
            vmem((nrows, inst), f32),
            vmem((nrows, inst), f32),
            vmem((nrows, inst), f32),
            vmem((ITERS, CHUNKS, part, inst), bf16),
            vmem((ITERS, 2, CHUNKS, part, inst), bf16),
            vmem((nrows, inst), f32),
            vmem((ITERS, CHUNKS, part, inst), bf16),
            vmem((ITERS, CHUNKS, part, inst), bf16),
            vmem((ITERS, CHUNKS, part, inst), f32),
            vmem((ITERS, CHUNKS, part, inst), f32),
            vmem((1, inst), f32),
            vmem((1, inst), f32),
            vmem((8, inst), f32),
            vmem((n, 8, inst), f32),
            vmem((ITERS, inst), f32),
            dma((14,)),
            dma((3,)),
            dma((ITERS, 2, CHUNKS)),
            dma((ITERS, 2, CHUNKS)),
            dma((ITERS, 2, CHUNKS)),
            dma((ITERS, 2, CHUNKS)),
            dma((n,)),
            dma((n,)),
            dma,
        ],
        compiler_params=pltpu.CompilerParams(
            collective_id=0, has_side_effects=True, vmem_limit_bytes=56 * 1024 * 1024
        ),
        cost_estimate=pl.CostEstimate(
            flops=4 * ITERS * nz * size * size * inst, bytes_accessed=6 * 2**20, transcendentals=0
        ),
    )(
        blocks,
        block_rows.reshape(1, nz),
        block_cols.reshape(1, nz),
        primal,
        dual,
        anchor_primal,
        anchor_dual,
        cost,
        rhs,
        bound_kind,
        lower.reshape(ncols // size, size),
        upper.reshape(ncols // size, size),
        step_size.reshape(1, inst),
        primal_weight.reshape(1, inst),
    )


def solution(mesh):
    return jax.shard_map(
        per_device,
        mesh=mesh,
        in_specs=(
            P("col", None, None),
            P("col"),
            P("col"),
            P("col", "groups"),
            P("col", "groups"),
            P("col", "groups"),
            P("col", "groups"),
            P("col", "groups"),
            P("col", "groups"),
            P("col", "groups"),
            P("col"),
            P("col"),
            P("groups"),
            P("groups"),
        ),
        out_specs=(P("col", "groups"), P("col", "groups"), P(None, "groups")),
        check_vma=False,
    )
```

time: 194 us -> 46.3 us (0.24)
  other arithmetic: 57 us -> 0 us
  Pallas kernels: 0 us -> 41.3 us
  waiting for transfers between devices: 30.9 us -> 0 us
  blocking collectives: 29.5 us -> 0 us
  starting transfers between devices: 26.9 us -> 0 us
  local copies, waits for them, and re-layouts: 29.8 us -> 4.12 us
  matrix products: 17.4 us -> 0 us
    pallas_call x0 -> x1, Pallas kernels: none -> 41.3 us  [per_device(): pl.pallas_call(functools.partial(kernel, n), out_shape=(jax.ShapeDtypeStr...]
    scatter-add x6 -> x0, other arithmetic: 40.3 us -> none  [the longest x3 20.2 us: per_device(): gradient = jnp.zeros((col_blocks, block_size, instances), jnp.float32).at...]
    ppermute x12 -> x0, waiting for transfers between devices: 30.9 us -> none  [the longest x6 25.6 us: from_behind(): return lax.ppermute(block, axis, route)]
    psum x1 -> x0, blocking collectives: 29.5 us -> none  [per_device(): lax.psum((jnp.stack(primal_terms), jnp.stack(dual_terms)), 'col')]
    ppermute x12 -> x0, starting transfers between devices: 26.9 us -> none  [the longest x3 13.9 us: padded(): after = lax.ppermute(leading, axis, down)]
    dot_general x6 -> x0, local copies, waits for them, and re-layouts: 21.4 us -> none  [the longest x3 10.7 us: per_device(): jnp.einsum('kji,kjb->kib', blocks, picked, preferred_element_type=jnp.flo...]
    dot_general x6 -> x0, matrix products: 17.4 us -> none  [the longest x3 9 us: per_device(): jnp.einsum('kij,kjb->kib', blocks, chosen, preferred_element_type=jnp.flo...]
    reduce_sum x6 -> x0, other arithmetic: 7.94 us -> none  [the longest x3 6.55 us: per_device(): primal_sq = jnp.sum((primal_next - current_x) ** 2, axis=0)]
  transfers between devices with their start and end apart: 12 -> 0, of which waited for: 8 -> 0; matrix products, arithmetic and copies ran while one was open for 2% -> 0% of each run, Pallas kernels for 0% -> 0%
where the time goes in v1:
time: 46.3 us; the launch traced here: 46.1 us
  Pallas kernels  41.3 us (89%)
  local copies, waits for them, and re-layouts  4.12 us (9%)
  between operations  0.65 us (1%)
    pallas_call x1, Pallas kernels, per_device(): pl.pallas_call(functools.partial(kernel, n), out_shape=(jax.ShapeDtypeStr...  41.3 us
    unnamed x5, local copies, waits for them, and re-layouts  4.12 us

profile of v1, /device:TPU:0, one launch (start us, length us, event | category | flops | bytes accessed | tf_op | source)
XLA Modules:
  0.0 46.1 jit_solution(17038027752277867834)
XLA Ops:
  0.6 41.3 %shard_map.157 = (f32[1024,128]{1,0:T(8,128)}, f32[512,128]{1,0:T(8,128)}, f32[3,128]{1,0:T(4,128)}) custom-call(bf16[48,128,128]{2,1,0:T(8,128)(2,1)} %blocks_hbm.1, s32[1,48]{1,0:T(1,128)} %bitcast.8, s32[1,48]{1,0:T(1,128)} %bitcast.9, f32[1024,128]{1,0:T(8,128)} %primal_hbm.1, f32[512,128]{1,0:T(8,128)} %dual_hbm.1, f32[1024,128]{1,0:T(8,128)} %anchor_primal_hbm.1, ...), custom_call_target="tpu_custom_call" | custom-call | flops 1207959552 | bytes 6291456 | tf_op jit(solution)/shard_map/pallas_call | solution.py:343
  42.0 0.0 copy-start
  42.0 1.9 %copy.20 = f32[1024,128]{1,0:T(8,128)} copy(f32[1024,128]{1,0:T(8,128)} %get-tuple-element.6) | data formatting | bytes 1048576
  43.9 1.7 %copy.21 = f32[512,128]{1,0:T(8,128)} copy(f32[512,128]{1,0:T(8,128)} %get-tuple-element.7) | data formatting | bytes 524288
  45.5 0.0 copy-done
  45.5 0.6 %copy.22 = f32[3,128]{1,0:T(4,128)} copy(f32[3,128]{1,0:T(4,128)S(1)} %copy-done) | data formatting | bytes 3072
Async XLA Ops:
  42.0 3.6 %copy-start = (f32[3,128]{1,0:T(4,128)S(1)}, f32[3,128]{1,0:T(4,128)}, u32[]{:S(2)}) copy-start(f32[3,128]{1,0:T(4,128)} %get-tuple-element.8) | copy-start | bytes 4612

commit v2 on v1

--- a/solution.py
+++ b/solution.py
@@ -40,7 +40,6 @@
     table,
     mat,
     mat_t,
-    x,
     x_next,
     anchor_x,
     cost,
@@ -51,7 +50,7 @@
     high_rows,
     grad,
     extra,
-    y,
+    base,
     anchor_y,
     rhs,
     own_y,
@@ -65,9 +64,7 @@
     weight,
     res_send,
     res_recv,
-    res,
     load_sem,
-    store_sem,
     halo_send_sem,
     halo_recv_sem,
     part_send_sem,
@@ -76,6 +73,7 @@
     res_recv_sem,
     table_sem,
 ):
+    x, y = primal_out, dual_out
     me = lax.axis_index("col")
     nz, size, _ = blocks_hbm.shape
     ncols, nrows = x.shape[0], y.shape[0]
@@ -97,9 +95,9 @@
     loads = {}
     for place, (name, source, target) in enumerate(
         (
-            ("y", dual_hbm, y),
             ("rows", rows_hbm, rows),
             ("cols", cols_hbm, cols),
+            ("y", dual_hbm, y),
             ("blocks", blocks_hbm, blk.at[pl.ds(1, nz)]),
             ("low", lower_hbm, low_rows),
             ("high", upper_hbm, high_rows),
@@ -138,17 +136,6 @@
             device_id_type=MESH,
         )
 
-    sent = []
-    loads["y"].wait()
-    for c in range(CHUNKS):
-        own_y[0, c] = y[c * part : (c + 1) * part].astype(jnp.bfloat16)
-    pl.semaphore_wait(barrier, n - 1)
-    for c in range(CHUNKS):
-        for who in (FAR, NEAR):
-            copy = halo_copy(0, who, c)
-            copy.start()
-            sent.append(copy)
-
     loads["rows"].wait()
     loads["cols"].wait()
     local_row = rows[...] - (me - 1) * row_blocks
@@ -165,12 +152,16 @@
     to_scalar = pltpu.make_async_copy(table_v, table, table_sem)
     to_scalar.start()
 
-    loads["low"].wait()
-    loads["high"].wait()
-    for c in range(col_blocks):
-        span = slice(c * size, (c + 1) * size)
-        low[span] = jnp.transpose(jnp.broadcast_to(low_rows[c : c + 1], (size, x.shape[1])))
-        high[span] = jnp.transpose(jnp.broadcast_to(high_rows[c : c + 1], (size, x.shape[1])))
+    sent = []
+    loads["y"].wait()
+    for c in range(CHUNKS):
+        own_y[0, c] = y[c * part : (c + 1) * part].astype(jnp.bfloat16)
+    pl.semaphore_wait(barrier, n - 1)
+    for c in range(CHUNKS):
+        for who in (FAR, NEAR):
+            copy = halo_copy(0, who, c)
+            copy.start()
+            sent.append(copy)
 
     blk[0] = jnp.zeros((size, size), jnp.bfloat16)
     blk_t[0] = jnp.zeros((size, size), jnp.bfloat16)
@@ -197,9 +188,16 @@
     loads["weight"].wait()
     primal_step = step[...] / weight[...]
     dual_step = step[...] * weight[...]
-    res_send[...] = jnp.zeros_like(res_send)
-    for name in ("x", "cost", "kind"):
+    for name in ("low", "high", "kind", "x", "cost"):
         loads[name].wait()
+    for c in range(col_blocks):
+        span = slice(c * size, (c + 1) * size)
+        of_kind = kind[span]
+        low_side = jnp.transpose(jnp.broadcast_to(low_rows[c : c + 1], (size, x.shape[1])))
+        high_side = jnp.transpose(jnp.broadcast_to(high_rows[c : c + 1], (size, x.shape[1])))
+        low[span] = jnp.where(of_kind == 0, -jnp.inf, low_side)
+        high[span] = jnp.where(of_kind == 2, high_side, jnp.inf)
+        base[span] = x[span] - primal_step * cost[span]
 
     def times(left, right):
         return jnp.dot(left, right, preferred_element_type=jnp.float32)
@@ -222,14 +220,10 @@
         for i in range(0, ncols, width):
             span = slice(i, i + width)
             total = grad[span] + times(mat_t[span, at : at + part], halo[turn, who, c])
-            now = x[span]
-            value = now - primal_step * (cost[span] - total)
-            of_kind = kind[span]
-            lower_only = jnp.maximum(value, low[span])
-            boxed = jnp.minimum(lower_only, high[span])
-            after = jnp.where(of_kind == 0, value, jnp.where(of_kind == 1, lower_only, boxed))
+            value = base[span] + primal_step * total
+            after = jnp.minimum(jnp.maximum(value, low[span]), high[span])
             x_next[span] = after
-            extra[span] = (2.0 * after - now).astype(jnp.bfloat16)
+            extra[span] = (2.0 * after - x[span]).astype(jnp.bfloat16)
 
         for who in (FAR, NEAR):
             for c in range(CHUNKS):
@@ -248,10 +242,10 @@
             span = slice(i, i + width)
             now, after = x[span], x_next[span]
             primal_sq += jnp.sum((after - now) ** 2, axis=0, keepdims=True)
-            x[span] = mixing * (2.0 * after - now) + (1.0 - mixing) * anchor_x[span]
-        if turn == ITERS - 1:
-            x_store = pltpu.make_async_copy(x, primal_out, store_sem.at[0])
-            x_store.start()
+            new = mixing * (2.0 * after - now) + (1.0 - mixing) * anchor_x[span]
+            x[span] = new
+            if turn < ITERS - 1:
+                base[span] = new - primal_step * cost[span]
 
         if turn == 0:
             loads["rhs"].wait()
@@ -294,8 +288,6 @@
         return carry
 
     lax.fori_loop(1, n, spread, 0)
-    y_store = pltpu.make_async_copy(y, dual_out, store_sem.at[1])
-    y_store.start()
     res_recv[0] = res_send[...]
     for copy in sent:
         copy.wait_send()
@@ -307,12 +299,7 @@
     lax.fori_loop(1, n, collect, 0)
     total = jnp.sum(res_recv[...], axis=0)
     cells = jnp.float32((ncols + nrows) * n)
-    res[...] = jnp.sqrt(total[0:ITERS] / cells)
-    res_store = pltpu.make_async_copy(res, residual_out, store_sem.at[2])
-    res_store.start()
-    x_store.wait()
-    y_store.wait()
-    res_store.wait()
+    residual_out[...] = jnp.sqrt(total / cells)
 
 
 def per_device(
@@ -343,12 +330,12 @@
     return pl.pallas_call(
         functools.partial(kernel, n),
         out_shape=(
-            jax.ShapeDtypeStruct((ncols, inst), f32),
-            jax.ShapeDtypeStruct((nrows, inst), f32),
-            jax.ShapeDtypeStruct((ITERS, inst), f32),
+            vmem((ncols, inst), f32),
+            vmem((nrows, inst), f32),
+            vmem((ITERS, inst), f32),
         ),
         in_specs=[any_space] * 14,
-        out_specs=(any_space,) * 3,
+        out_specs=(pl.BlockSpec(memory_space=vmem),) * 3,
         scratch_shapes=[
             vmem((nz + 1, size, size), bf16),
             vmem((nz + 1, size, size), bf16),
@@ -361,7 +348,6 @@
             vmem((ncols, inst), f32),
             vmem((ncols, inst), f32),
             vmem((ncols, inst), f32),
-            vmem((ncols, inst), f32),
             vmem((ncols, inst), i32),
             vmem((ncols, inst), f32),
             vmem((ncols, inst), f32),
@@ -369,7 +355,7 @@
             vmem((ncols // size, size), f32),
             vmem((ncols, inst), f32),
             vmem((ncols, inst), bf16),
-            vmem((nrows, inst), f32),
+            vmem((ncols, inst), f32),
             vmem((nrows, inst), f32),
             vmem((nrows, inst), f32),
             vmem((ITERS, CHUNKS, part, inst), bf16),
@@ -381,11 +367,9 @@
             vmem((ITERS, CHUNKS, part, inst), f32),
             vmem((1, inst), f32),
             vmem((1, inst), f32),
-            vmem((8, inst), f32),
-            vmem((n, 8, inst), f32),
             vmem((ITERS, inst), f32),
+            vmem((n, ITERS, inst), f32),
             dma((14,)),
-            dma((3,)),
             dma((ITERS, 2, CHUNKS)),
             dma((ITERS, 2, CHUNKS)),
             dma((ITERS, 2, CHUNKS)),

time: 46.3 us -> 43.1 us (0.931)
  local copies, waits for them, and re-layouts: 4.12 us -> 2.08 us
  Pallas kernels: 41.3 us -> 40.2 us
    unnamed x5 -> x3, local copies, waits for them, and re-layouts: 4.12 us -> 2.08 us
    pallas_call x1, Pallas kernels: 41.3 us -> 40.2 us  [per_device(): pl.pallas_call(functools.partial(kernel, n), out_shape=(vmem((ncols, inst...]
where the time goes in v2:
time: 43.1 us; the launch traced here: 42.9 us
  Pallas kernels  40.2 us (93%)
  local copies, waits for them, and re-layouts  2.08 us (5%)
  between operations  0.65 us (2%)
    pallas_call x1, Pallas kernels, per_device(): pl.pallas_call(functools.partial(kernel, n), out_shape=(vmem((ncols, inst...  40.2 us
    unnamed x3, local copies, waits for them, and re-layouts  2.08 us

profile of v2, /device:TPU:0, one launch (start us, length us, event | category | flops | bytes accessed | tf_op | source)
XLA Modules:
  0.0 42.9 jit_solution(12713483158591131497)
XLA Ops:
  0.6 40.2 %shard_map.157 = (f32[1024,128]{1,0:T(8,128)S(1)}, f32[512,128]{1,0:T(8,128)S(1)}, f32[3,128]{1,0:T(4,128)S(1)}) custom-call(bf16[48,128,128]{2,1,0:T(8,128)(2,1)} %blocks_hbm.1, s32[1,48]{1,0:T(1,128)} %bitcast.8, s32[1,48]{1,0:T(1,128)} %bitcast.9, f32[1024,128]{1,0:T(8,128)} %primal_hbm.1, f32[512,128]{1,0:T(8,128)} %dual_hbm.1, ...), custom_call_target="tpu_custom_call" | custom-call | flops 1207959552 | bytes 6291456 | tf_op jit(solution)/shard_map/pallas_call | solution.py:330
  40.9 0.8 %copy.20 = f32[1024,128]{1,0:T(8,128)} copy(f32[1024,128]{1,0:T(8,128)S(1)} %get-tuple-element.3) | data formatting | bytes 1048576
  41.7 0.6 %copy.22 = f32[3,128]{1,0:T(4,128)} copy(f32[3,128]{1,0:T(4,128)S(1)} %get-tuple-element.5) | data formatting | bytes 3072
  42.2 0.7 %copy.21 = f32[512,128]{1,0:T(8,128)} copy(f32[512,128]{1,0:T(8,128)S(1)} %get-tuple-element.4) | data formatting | bytes 524288

commit v3 on v2

--- a/solution.py
+++ b/solution.py
@@ -284,7 +284,7 @@
         )
 
     def spread(k, carry):
-        res_copy(k).start()
+        res_copy(lax.rem(k + n // 2 - 1, n - 1) + 1).start()
         return carry
 
     lax.fori_loop(1, n, spread, 0)

time: 43.1 us -> 43.3 us (level)
  no operation moved by 1% of the time
where the time goes in v3:
time: 43.3 us; the launch traced here: 43.1 us
  Pallas kernels  40.4 us (93%)
  local copies, waits for them, and re-layouts  2.08 us (5%)
  between operations  0.65 us (2%)
    pallas_call x1, Pallas kernels, per_device(): pl.pallas_call(functools.partial(kernel, n), out_shape=(vmem((ncols, inst...  40.4 us
    unnamed x3, local copies, waits for them, and re-layouts  2.08 us

profile of v3, /device:TPU:0, one launch (start us, length us, event | category | flops | bytes accessed | tf_op | source)
XLA Modules:
  0.0 43.1 jit_solution(2256867893468899108)
XLA Ops:
  0.6 40.4 %shard_map.157 = (f32[1024,128]{1,0:T(8,128)S(1)}, f32[512,128]{1,0:T(8,128)S(1)}, f32[3,128]{1,0:T(4,128)S(1)}) custom-call(bf16[48,128,128]{2,1,0:T(8,128)(2,1)} %blocks_hbm.1, s32[1,48]{1,0:T(1,128)} %bitcast.8, s32[1,48]{1,0:T(1,128)} %bitcast.9, f32[1024,128]{1,0:T(8,128)} %primal_hbm.1, f32[512,128]{1,0:T(8,128)} %dual_hbm.1, ...), custom_call_target="tpu_custom_call" | custom-call | flops 1207959552 | bytes 6291456 | tf_op jit(solution)/shard_map/pallas_call | solution.py:330
  41.0 0.8 %copy.20 = f32[1024,128]{1,0:T(8,128)} copy(f32[1024,128]{1,0:T(8,128)S(1)} %get-tuple-element.3) | data formatting | bytes 1048576
  41.8 0.6 %copy.22 = f32[3,128]{1,0:T(4,128)} copy(f32[3,128]{1,0:T(4,128)S(1)} %get-tuple-element.5) | data formatting | bytes 3072
  42.4 0.7 %copy.21 = f32[512,128]{1,0:T(8,128)} copy(f32[512,128]{1,0:T(8,128)S(1)} %get-tuple-element.4) | data formatting | bytes 524288
